TPU v7x, 32 devices: a whole 2x2x4 slice. The times are simulated.
32 devices in a mesh: layer: 4 (over x, core), dp: 8 (over z, y).
Axes of the slice: x: 2, y: 2, z: 4, core: 2. Of those that a mesh axis runs over, the one named last changes fastest.
Arguments:
- acts: bfloat16 [4, 2048, 4096], P('layer', 'dp'), may hold values from -6 to 6
- factor_old: bfloat16 [4, 4096, 4096], P('layer', 'dp'), as said below
- basis_old: bfloat16 [4, 4096, 256], P('layer', 'dp'), may hold values from -0.09375 to 0.09375
- grads: bfloat16 [4, 4096, 2048], P(None, 'dp', 'layer'), may hold values from -12 to 12
Outputs:
- new_basis: bfloat16 [4, 4096, 256], P('layer', 'dp')
- eigenvalues: bfloat16 [4, 256], P('layer')
- preconditioned: bfloat16 [4, 4096, 2048], P(None, 'dp', 'layer')
- applied_rows: float32 [4, 4096, 256], P('layer', 'dp')
Inputs may be any that keep to these rules, and one draw needn't show every extreme that they name: `factor_old`: each block is symmetric with a positive diagonal that outweighs the spectral norm of its off-diagonal part.
All inputs are finite; a program needn't handle non-finite values.
Results may differ from a plain program's by a relative error of at most 0.0035.
Values may be sent and summed in bfloat16 or wider, within the bound.
A program may use at most 64 MiB of HBM per device.

v0:
```python
import math

import jax
import jax.numpy as jnp
from jax import lax
from jax.sharding import PartitionSpec as P

decay_rate = 0.25
damping = 2.0


def per_device(acts, factor_old, basis_old, grads):
    old_basis = lax.all_gather(basis_old, "dp", axis=1, tiled=True)[0]
    token_rows = acts[0]
    projected = jnp.dot(token_rows, old_basis, preferred_element_type=jnp.float32).astype(
        jnp.bfloat16
    )
    summed = lax.psum_scatter(
        lax.dot_general(
            token_rows, projected, (((0,), (0,)), ((), ())), preferred_element_type=jnp.float32
        ),
        "dp",
        scatter_dimension=0,
        tiled=True,
    )
    total_tokens = token_rows.shape[0] * lax.axis_size("dp")
    applied = (
        decay_rate * jnp.dot(factor_old[0], old_basis, preferred_element_type=jnp.float32)
        + (1.0 - decay_rate) / total_tokens * summed
    )
    applied_rows = applied * math.sqrt(factor_old.shape[2])
    gram_local = jnp.dot(applied.T, applied, precision=lax.Precision.HIGHEST)
    gram_total = lax.psum(gram_local, "dp")
    lower = jnp.linalg.cholesky(gram_total)
    eigen_vals = jnp.diagonal(lower).astype(jnp.bfloat16)
    solved = lax.linalg.triangular_solve(
        lower, applied, left_side=False, lower=True, transpose_a=True
    )
    fresh = solved.astype(jnp.bfloat16)
    slab = lax.all_to_all(grads, "layer", split_axis=0, concat_axis=2, tiled=True)[0]
    coupling_local = lax.dot_general(
        fresh, slab, (((0,), (0,)), ((), ())), preferred_element_type=jnp.float32
    )
    coupling = lax.psum(coupling_local, "dp")
    factors = 1.0 / (eigen_vals.astype(jnp.float32) + damping) - 1.0 / damping
    scaled = (factors[:, None] * coupling).astype(jnp.bfloat16)
    result = slab.astype(jnp.float32) / damping + jnp.dot(
        fresh, scaled, preferred_element_type=jnp.float32
    )
    conditioned = lax.all_to_all(
        result.astype(jnp.bfloat16)[None], "layer", split_axis=2, concat_axis=0, tiled=True
    )
    return (fresh[None], eigen_vals[None], conditioned, applied_rows[None])


def solution(mesh):
    in_specs = (
        P("layer", "dp", None),
        P("layer", "dp", None),
        P("layer", "dp", None),
        P(None, "dp", "layer"),
    )
    out_specs = (
        P("layer", "dp", None),
        P("layer", None),
        P(None, "dp", "layer"),
        P("layer", "dp", None),
    )
    return jax.shard_map(
        per_device, mesh=mesh, in_specs=in_specs, out_specs=out_specs, check_vma=False
    )
```

profile of v0, /device:TPU:0, one launch (start us, length us, event | category | flops | bytes accessed | tf_op | source)
XLA Modules:
  0.0 484.7 jit_solution(16953100787019699989)
XLA Ops:
  8.0 54.2 %all-gather.2.cloned.1.call-done = bf16[1,4096,256]{2,1,0:T(8,128)(2,1)} async-done(((bf16[1,512,256]{2,1,0:T(8,128)(2,1)}), bf16[1,4096,256]{2,1,0:T(8,128)(2,1)}) %all-gather.2.cloned.1.call-update) | async-done | bytes 2097168 | tf_op jit(solution)/shard_map/all_gather | solution.py:13
  62.2 5.9 %convolution_bitcast_fusion = f32[4096,256]{1,0:T(8,128)} fusion(bf16[1,256,4096]{2,1,0:T(8,128)(2,1)S(1)} %copy-done, bf16[1,4096,256]{2,1,0:T(8,128)(2,1)} %all-gather.2.cloned.1.call-done), kind=kOutput, calls=%fused_computation.3 | convolution fusion | flops 1073807360 | bytes 8388608 | tf_op jit(solution)/shard_map/dot_general | solution.py:19
  68.1 4.5 all-to-all-start
  72.7 82.2 %reduce-scatter.2.cloned.1.call-done = f32[512,256]{1,0:T(8,128)} async-done(((f32[4096,256]{1,0:T(8,128)}), f32[512,256]{1,0:T(8,128)}) %reduce-scatter.2.cloned.1.call-update) | async-done | bytes 524304 | tf_op jit(solution)/shard_map/reduce_scatter | solution.py:18
  154.8 4.1 fusion.13
  161.0 3.2 copy.30
  166.2 65.0 %all-reduce.4.cloned.1.call-done = f32[256,256]{0,1:T(8,128)} async-done(((f32[256,256]{0,1:T(8,128)}), f32[256,256]{0,1:T(8,128)}) %all-reduce.4.cloned.1.call-update) | async-done | bytes 262160 | tf_op jit(solution)/shard_map/psum | solution.py:33
  233.3 11.7 %cholesky.50 = f32[128,128]{1,0:T(8,128)S(1)} custom-call(f32[128,128]{1,0:T(8,128)S(1)} %cholesky.118), custom_call_target="Cholesky" | custom-call | tf_op jit(solution)/shard_map/jit(cholesky)/cholesky | solution.py:34
  245.0 9.8 %custom-call.14 = f32[1,128,128]{1,2,0:T(8,128)S(1)} custom-call(f32[1,128,128]{2,1,0:T(8,128)S(1)} %get-tuple-element.43), custom_call_target="InvertDiagBlocksLowerTriangular" | custom-call | tf_op jit(solution)/shard_map/jit(cholesky)/cholesky | solution.py:34
  255.3 11.9 %cholesky.105 = f32[128,128]{1,0:T(8,128)S(1)} custom-call(f32[128,128]{1,0:T(8,128)S(1)} %convolution_subtract_fusion.1), custom_call_target="Cholesky" | custom-call | tf_op jit(solution)/shard_map/jit(cholesky)/cholesky | solution.py:34
  269.3 4.0 while.1
  273.3 19.7 %custom-call.15 = f32[2,128,128]{1,2,0:T(8,128)S(1)} custom-call(f32[2,128,128]{2,1,0:T(8,128)S(1)} %get-tuple-element.11), custom_call_target="InvertDiagBlocksLowerTriangular" | custom-call | tf_op jit(solution)/shard_map/triangular_solve | solution.py:36
  294.4 3.6 fusion.32
  298.1 2.5 gather_fusion
  300.6 98.7 %all-reduce.6.cloned.1.call-done = f32[256,2048]{1,0:T(8,128)} async-done(((f32[256,2048]{1,0:T(8,128)}), f32[256,2048]{1,0:T(8,128)}) %all-reduce.6.cloned.1.call-update) | async-done | bytes 2097168 | tf_op jit(solution)/shard_map/psum | solution.py:44
  399.3 4.4 fusion.2
  403.6 10.8 %copy.31 = bf16[1,512,2048]{1,0,2:T(2,128)(2,1)} copy(bf16[1,512,2048]{2,1,0:T(8,128)(2,1)} %fusion.2) | data formatting | bytes 4194304 | tf_op jit(solution)/shard_map/broadcast_in_dim | solution.py:51
  414.9 15.4 %reduce.12 = bf16[2048,512]{1,0:T(8,128)(2,1)} reduce(bf16[2048,1,512]{2,1,0:T(2,128)(2,1)} %bitcast.89, bf16[]{:T(256)} %broadcast.146), dimensions={1}, to_apply=%bitcast.68.reduce_sub_computation | reduce | bytes 4194306
  430.3 4.5 reshape.97
  434.8 4.4 all-to-all-start.1
  441.5 23.5 %all-to-all-done.1 = bf16[4,2,131072]{2,1,0:T(2,128)(2,1)} async-done(((bf16[4,2,131072]{2,1,0:T(2,128)(2,1)}), bf16[4,2,131072]{2,1,0:T(2,128)(2,1)}, u32[]{:S(2)}, u32[]{:S(2)}) %all-to-all-start.1) | async-done | bytes 2097184 | tf_op jit(solution)/shard_map/all_to_all | solution.py:50
  465.0 5.0 %reshape.98 = bf16[2048,1,512]{2,1,0:T(2,128)(2,1)} reshape(bf16[4,2,131072]{2,1,0:T(2,128)(2,1)} %all-to-all-done.1) | data formatting | bytes 4194304
  470.0 4.1 copy.36
  474.1 4.1 copy.33
  (42 shorter events, 16.3 us)
Async XLA Ops:
  7.2 55.0 %copy-start = (bf16[1,256,4096]{2,1,0:T(8,128)(2,1)S(1)}, bf16[1,256,4096]{2,1,0:T(8,128)(2,1)}, u32[]{:S(2)}) copy-start(bf16[1,256,4096]{2,1,0:T(8,128)(2,1)} %param.4) | copy-start | bytes 6291460
  7.2 55.0 %all-gather.2.cloned.1.call-start = ((), (), s32[]{:S(2)}) async-start(), calls=%async_computation.3 | async-start | bytes 2359296 | tf_op jit(solution)/shard_map/all_gather | solution.py:13
  7.9 146.9 %reduce-scatter.2.cloned.1.call-start = ((), (), s32[]{:S(2)}) async-start(), calls=%async_computation.4 | async-start | bytes 4718592 | tf_op jit(solution)/shard_map/reduce_scatter | solution.py:18
  68.1 92.8 %all-to-all-start = ((bf16[4,512,512]{2,1,0:T(8,128)(2,1)}), bf16[4,512,512]{2,1,0:T(8,128)(2,1)}, u32[]{:S(2)}, u32[]{:S(2)}) async-start(bf16[4,512,512]{2,1,0:T(8,128)(2,1)} %param.7), calls=%async_computation.1 | async-start | bytes 4194304 | tf_op jit(solution)/shard_map/all_to_all | solution.py:40
  72.6 158.6 %all-reduce.4.cloned.1.call-start = ((), (), s32[]{:S(2)}) async-start(), calls=%async_computation.5 | async-start | bytes 524288 | tf_op jit(solution)/shard_map/psum | solution.py:33
  160.7 238.6 %all-reduce.6.cloned.1.call-start = ((), (), s32[]{:S(2)}) async-start(), calls=%async_computation.6 | async-start | bytes 4194304 | tf_op jit(solution)/shard_map/psum | solution.py:44
  434.8 30.2 %all-to-all-start.1 = ((bf16[4,2,131072]{2,1,0:T(2,128)(2,1)}), bf16[4,2,131072]{2,1,0:T(2,128)(2,1)}, u32[]{:S(2)}, u32[]{:S(2)}) async-start(bf16[4,2,131072]{2,1,0:T(2,128)(2,1)} %reshape.97), calls=%async_computation.2 | async-start | bytes 4194304 | tf_op jit(solution)/shard_map/all_to_all | solution.py:50
Sparse Core Ops, SparseCore 0:
  10.1 51.9 all-gather.1
  68.3 86.5 reduce-scatter.1
  160.9 70.2 all-reduce.3
  298.2 101.0 all-reduce.5
where the time goes:
time: 486 us; the launch traced here: 485 us
  waiting for transfers between devices  324 us (67%)
  other arithmetic  71.1 us (15%)
  local copies, waits for them, and re-layouts  43.1 us (9%)
  matrix products  21.7 us (4%)
  between operations  15.2 us (3%)
  starting transfers between devices  9.25 us (2%)
    psum x1, waiting for transfers between devices, per_device(): coupling = lax.psum(coupling_local, 'dp')  98.7 us
    reduce_scatter x1, waiting for transfers between devices, per_device(): lax.psum_scatter(lax.dot_general(token_rows, projected, (((0,), (0,)), ((...  82.2 us
    psum x1, waiting for transfers between devices, per_device(): gram_total = lax.psum(gram_local, 'dp')  65 us
    all_gather x1, waiting for transfers between devices, per_device(): old_basis = lax.all_gather(basis_old, 'dp', axis=1, tiled=True)[0]  54.2 us
    another operation x6, other arithmetic, per_device(): lower = jnp.linalg.cholesky(gram_total)  34.1 us
    all_to_all x1, waiting for transfers between devices, per_device(): lax.all_to_all(result.astype(jnp.bfloat16)[None], 'layer', split_axis=2,...  23.5 us
    unnamed x9, local copies, waits for them, and re-layouts  21 us
    another operation x4, other arithmetic, per_device(): lax.linalg.triangular_solve(lower, applied, left_side=False, lower=True,...  19.7 us
  transfers between devices with their start and end apart: 6, of which 5 were waited for; matrix products, arithmetic and copies ran while one was open for 3% of the time, Pallas kernels for 0%

commit v1 on v0

v1 whole, which is shorter than its diff:
```python
import functools
import math

import jax
import jax.numpy as jnp
from jax import lax
from jax.experimental import pallas as pl
from jax.experimental.pallas import tpu as pltpu
from jax.sharding import PartitionSpec as P

decay_rate = 0.25
damping = 2.0
PANEL = 32
HIGHEST = lax.Precision.HIGHEST
F32 = jnp.float32
BF16 = jnp.bfloat16


def loop(count, body):
    if count <= 4:
        for i in range(count):
            body(i)
    elif count > 0:

        def step(i, carry):
            body(i)
            return carry

        lax.fori_loop(0, count, step, 0)


def dot_nn(a, b, **kw):
    return lax.dot_general(a, b, (((1,), (0,)), ((), ())), preferred_element_type=F32, **kw)


def dot_tn(a, b, **kw):
    return lax.dot_general(a, b, (((0,), (0,)), ((), ())), preferred_element_type=F32, **kw)


def dot_nt(a, b, **kw):
    return lax.dot_general(a, b, (((1,), (1,)), ((), ())), preferred_element_type=F32, **kw)


def pieces(value):
    high = value.astype(BF16)
    rest = value - high.astype(F32)
    mid = rest.astype(BF16)
    return high, mid, (rest - mid.astype(F32)).astype(BF16)


def narrow_nn(a, b):
    ah, am, al = pieces(a)
    bh, bm, bl = pieces(b)
    return dot_nn(
        jnp.concatenate([ah, ah, am, ah, al, am], axis=1),
        jnp.concatenate([bh, bm, bh, bl, bh, bm], axis=0),
    )


def narrow_nt(a, b):
    ah, am, al = pieces(a)
    bh, bm, bl = pieces(b)
    return dot_nt(
        jnp.concatenate([ah, ah, am, ah, al, am], axis=1),
        jnp.concatenate([bh, bm, bh, bl, bh, bm], axis=1),
    )


def panel_factor(block, n):
    rows = lax.broadcasted_iota(jnp.int32, (n, n), 0)
    cols = lax.broadcasted_iota(jnp.int32, (n, n), 1)
    x = jnp.concatenate([block, (rows == cols).astype(F32)], axis=1)
    tile = (8, 2 * n)
    row = lax.broadcasted_iota(jnp.int32, tile, 0)
    tiles = [x[t : t + 8, :] for t in range(0, n, 8)]
    pivots = [jnp.ones(tile, F32) for _ in tiles]
    for j in range(0, n, 4):
        own, sub = j // 8, j % 8
        live = range(own, n // 8)
        c = [{t: jnp.broadcast_to(tiles[t][:, j + m : j + m + 1], tile) for t in live} for m in range(4)]
        r = [jnp.broadcast_to(tiles[own][sub + m : sub + m + 1, :], tile) for m in range(4)]
        p = {
            (i, m): jnp.broadcast_to(c[m][own][sub + i : sub + i + 1, :], tile)
            for m in range(4)
            for i in range(m, 4)
        }
        change = {t: None for t in live}
        for m in range(4):
            pivots[own] = jnp.where(row == sub + m, p[m, m], pivots[own])
            inv = 1.0 / p[m, m]
            scaled = r[m] * inv
            for t in live:
                column = jnp.where(row > sub + m, c[m][t], 0.0) if t == own else c[m][t]
                change[t] = column * scaled if change[t] is None else change[t] + column * scaled
            for i in range(m + 1, 4):
                f = p[i, m] * inv
                for q in range(m + 1, i + 1):
                    p[i, q] = p[i, q] - f * p[q, m]
                r[i] = r[i] - f * r[m]
                for t in live:
                    c[i][t] = c[i][t] - f * c[m][t]
        for t in live:
            tiles[t] = tiles[t] - change[t]
    root = [jnp.sqrt(d) for d in pivots]
    inverse = jnp.concatenate([t / d for t, d in zip(tiles, root)], axis=0)[:, n:]
    return jnp.concatenate(root, axis=0)[:, :1], inverse


def cholesky_step(k, found, aug, roots, done):
    order, width = aug.shape
    root, inverse = found
    here = pl.ds(pl.multiple_of(k * PANEL, PANEL), PANEL)
    after = jnp.minimum(k + 1, order // PANEL - 1)
    below = pl.ds(pl.multiple_of(after * PANEL, PANEL), PANEL)
    roots[here, :] = root
    mine = aug[here, :]
    next_rows = aug[below, : 2 * PANEL]
    next_left = narrow_nt(next_rows[:, :PANEL], inverse)
    next_strip = narrow_nn(inverse, mine[:, PANEL : 2 * PANEL])
    ahead = panel_factor(next_rows[:, PANEL:] - narrow_nn(next_left, next_strip), PANEL)
    strip = narrow_nn(inverse, mine)
    lower = lax.broadcasted_iota(jnp.int32, (order, 1), 0) >= (k + 1) * PANEL
    left = jnp.where(lower, narrow_nt(aug[:, :PANEL], inverse), 0.0)
    aug[...] = aug[...] - narrow_nn(left, strip)
    aug[here, :] = strip
    done(k, root, pltpu.roll(strip, width - order + k * PANEL, 1)[:, :order])
    aug[...] = pltpu.roll(aug[...], width - PANEL, 1)
    return ahead


def finish_kernel(
    mall, cfull, appall, grads, applied, new_basis, eigen, out, fresh, rows, eigen_out, *, scale
):
    rank = applied.shape[1]
    scaled = dot_nn(mall[0, :, 1].reshape(rank, rank), cfull[...].reshape(rank, cfull.shape[2])).astype(BF16)
    scaled = dot_tn(mall[0, :, 0].reshape(rank, rank), scaled).astype(BF16)
    out[0] = (grads[0].astype(F32) / damping + dot_nn(appall[0], scaled)).astype(BF16)

    @pl.when(pl.program_id(0) == 0)
    def _():
        fresh[...] = new_basis[...]
        rows[...] = applied[...] * scale
        eigen_out[...] = eigen[...].astype(BF16)


def kernel(
    layers, Z, Y, token_total,
    acts_hbm, factor_hbm, basis_hbm, grads_hbm,
    mall, cfull, appall, applied_ref, fresh_ref, eigen_ref,
    acts, factor, grads, qfull, projected, fq,
    ysend_a, ybuf_a, zsend_a, zbuf_a,
    gpart, gbuf, gfull, aug, roots,
    c0p, ysend_c, ybuf_c, zsend_c, zbuf_c,
    load_sem,
    ag_z, ag_y, ag_zf, ag_yf, ag_recv,
    ys_a, yr_a, zs_a, zr_a,
    lay_send, lay_recv,
    gs_send, gs_recv, gg_send, gg_recv,
    ys_c, yr_c, zs_c, zr_c,
    cg_z, cg_y, cg_zf, cg_yf, cg_recv,
    m_send, m_recv,
):
    ag = (ag_z, ag_y, ag_zf, ag_yf, ag_recv)
    cg = (cg_z, cg_y, cg_zf, cg_yf, cg_recv)
    layer = lax.axis_index("layer")
    me = lax.axis_index("dp")
    z, y = me // Y, me % Y
    dp = Z * Y
    rows = factor.shape[0]
    rank = qfull.shape[2]
    zorder = [2, 1, 3] if Z == 4 else list(range(1, Z))

    def zpeer(k):
        return lax.rem(z + k, Z)

    def ypeer(j):
        return lax.rem(y + j, Y)

    def send(src, dst, ssem, rsem, **where):
        return pltpu.make_async_remote_copy(
            src_ref=src, dst_ref=dst, send_sem=ssem, recv_sem=rsem,
            device_id=where, device_id_type=pl.DeviceIdType.MESH,
        )

    loads = [
        pltpu.make_async_copy(src, dst, load_sem.at[i])
        for i, (src, dst) in enumerate(
            [
                (basis_hbm.at[0], qfull.at[me]),
                (acts_hbm.at[0], acts),
                (factor_hbm.at[0], factor),
                (grads_hbm, grads),
            ]
        )
    ]
    for load in loads:
        load.start()

    barrier = pltpu.get_barrier_semaphore()

    def greet_dp(i):
        pl.semaphore_signal(
            barrier, inc=1, device_id={"dp": lax.rem(me + 1 + i, dp)}, device_id_type=pl.DeviceIdType.MESH
        )

    def greet_layer(i):
        pl.semaphore_signal(
            barrier, inc=1, device_id={"layer": lax.rem(layer + 1 + i, layers)}, device_id_type=pl.DeviceIdType.MESH
        )

    loop(dp - 1, greet_dp)
    loop(layers - 1, greet_layer)
    pl.semaphore_wait(barrier, dp - 1 + layers - 1)

    def arrived(full, s, sems):
        send(full.at[s], full.at[s], sems[0].at[0], sems[4].at[s], dp=lax.rem(me + 1, dp)).wait_recv()

    def own_sends(full, sems, act):
        for i, side in enumerate((-1, 1)):
            @pl.when((z + side >= 0) & (z + side < Z))
            def _():
                act(send(full.at[me], full.at[me], sems[0].at[i], sems[4].at[me], dp=(z + side) * Y + y))

        def to_y(j):
            act(send(full.at[me], full.at[me], sems[1].at[j], sems[4].at[me], dp=z * Y + ypeer(j + 1)))

        loop(Y - 1, to_y)

    def passed_on(full, sems, dist, act, before=None, after=None):
        for i, side in enumerate((-1, 1)):
            @pl.when((z + side * dist >= 0) & (z + side * dist < Z))
            def _():
                s = (z + side * dist) * Y + y
                if before is not None:
                    before(s)

                @pl.when((z - side >= 0) & (z - side < Z))
                def _():
                    act(
                        send(
                            full.at[s], full.at[s], sems[2].at[i, dist - 1], sems[4].at[s], dp=(z - side) * Y + y
                        )
                    )

                def forward(j):
                    act(
                        send(
                            full.at[s], full.at[s], sems[3].at[i, dist - 1, j], sems[4].at[s],
                            dp=z * Y + ypeer(j + 1),
                        )
                    )

                loop(Y - 1, forward)
                if after is not None:
                    after(s)

    def gather_start(full, sems):
        own_sends(full, sems, lambda copy: copy.start())

    def gather_stage(full, sems, dist, use=None):
        passed_on(full, sems, dist, lambda copy: copy.start(), lambda s: arrived(full, s, sems), use)

    def gather_rows(full, sems, use):
        def take_row(zs):
            def take(j):
                s = zs * Y + ypeer(j + 1)
                arrived(full, s, sems)
                use(s)

            loop(Y - 1, take)

        take_row(z)
        for dist in range(1, Z):
            for side in (-1, 1):
                @pl.when((z + side * dist >= 0) & (z + side * dist < Z))
                def _():
                    take_row(z + side * dist)

    def gather_done(full, sems):
        own_sends(full, sems, lambda copy: copy.wait_send())
        for dist in range(1, Z):
            passed_on(full, sems, dist, lambda copy: copy.wait_send())

    korder = zorder + [0]

    def y_copy(k, j, ysend, ybuf, ys, yr):
        return send(
            ysend.at[k, j], ybuf.at[k, j], ys.at[k, j], yr.at[k, j], dp=z * Y + ypeer(j + 1)
        )

    def z_copy(k, zsend, zbuf, zs, zr):
        return send(zsend.at[k - 1], zbuf.at[k - 1], zs.at[k - 1], zr.at[k - 1], dp=zpeer(k) * Y + y)

    def scatter_y(produce, ysend, ybuf, ys, yr):
        for k in korder:

            def body(j):
                ysend[k, j] = produce(zpeer(k) * Y + ypeer(j + 1)).astype(BF16)
                y_copy(k, j, ysend, ybuf, ys, yr).start()

            loop(Y - 1, body)

    def scatter_z(produce, ysend, ybuf, ys, yr, zsend, zbuf, zs, zr):
        total = None
        for k in korder:
            total = produce(zpeer(k) * Y + y)
            for j in range(Y - 1):
                y_copy(k, j, ysend, ybuf, ys, yr).wait_recv()
                total = total + ybuf[k, j].astype(F32)
            if k > 0:
                zsend[k - 1] = total.astype(BF16)
                z_copy(k, zsend, zbuf, zs, zr).start()
        return total

    def scatter_sum(total, zsend, zbuf, zs, zr):
        for k in range(1, Z):
            z_copy(k, zsend, zbuf, zs, zr).wait_recv()
            total = total + zbuf[k - 1].astype(F32)
        return total

    def scatter_done(ysend, ybuf, ys, yr, zsend, zbuf, zs, zr):
        for k in range(Z):
            loop(Y - 1, lambda j: y_copy(k, j, ysend, ybuf, ys, yr).wait_send())
        for k in range(1, Z):
            z_copy(k, zsend, zbuf, zs, zr).wait_send()

    loads[0].wait()
    gather_start(qfull, ag)
    loads[1].wait()
    loads[2].wait()

    def columns(s):
        return pl.ds(pl.multiple_of(s * rows, rows), rows)

    def use_basis(s):
        block = qfull[s]
        projected[...] += dot_nn(acts[:, columns(s)], block)
        fq[...] += dot_nn(factor[:, columns(s)], block)

    own = qfull[me]
    projected[...] = dot_nn(acts[:, columns(me)], own)
    fq[...] = dot_nn(factor[:, columns(me)], own)
    for dist in range(1, Z):
        gather_stage(qfull, ag, dist, use_basis)
    gather_rows(qfull, ag, use_basis)

    short = projected[...].astype(BF16)

    def token_part(s):
        return dot_tn(acts[:, columns(s)], short)

    scatter_y(token_part, ysend_a, ybuf_a, ys_a, yr_a)
    total = scatter_z(token_part, ysend_a, ybuf_a, ys_a, yr_a, zsend_a, zbuf_a, zs_a, zr_a)
    total = scatter_sum(total, zsend_a, zbuf_a, zs_a, zr_a)
    applied = decay_rate * fq[...] + (1.0 - decay_rate) / token_total * total
    applied_ref[...] = applied
    appall[layer] = applied.astype(BF16)

    pair, core = layer // 2, layer % 2
    pairs = layers // 2
    partner = pair * 2 + 1 - core

    def same_core(i):
        return lax.rem(pair + 1 + i, pairs) * 2 + core

    def layer_own(act):
        act(send(appall.at[layer], appall.at[layer], lay_send.at[pairs - 1], lay_recv.at[layer], layer=partner))

        def out(i):
            act(send(appall.at[layer], appall.at[layer], lay_send.at[i], lay_recv.at[layer], layer=same_core(i)))

        loop(pairs - 1, out)

    def layer_pass(i, act):
        b = same_core(i)
        act(send(appall.at[b], appall.at[b], lay_send.at[pairs + i], lay_recv.at[b], layer=partner))

    def layer_wait(b):
        send(appall.at[b], appall.at[b], lay_send.at[0], lay_recv.at[b], layer=partner).wait_recv()

    layer_own(lambda copy: copy.start())

    gpart[...] = dot_tn(applied, applied, precision=HIGHEST)
    strip = rank // dp

    def strip_of(s):
        return pl.ds(pl.multiple_of(s * strip, strip), strip)

    def strip_copy(i):
        to = lax.rem(me + 1 + i, dp)
        return send(gpart.at[strip_of(to)], gbuf.at[me], gs_send.at[i], gs_recv.at[me], dp=to)

    loop(dp - 1, lambda i: strip_copy(i).start())

    chunk = cfull.shape[1]
    per = rank // chunk

    def coupling_chunk(s):
        return c0p[pl.ds(pl.multiple_of(s * chunk, chunk), chunk), :]

    def coupling_part(b):
        c0p[pl.ds(pl.multiple_of(b * rank, rank), rank), :] = dot_tn(appall[b], grads[b])
        for i in range(per):
            s = b * per + i
            k = lax.rem(s // Y - z + Z, Z)
            j = lax.rem(s % Y - y + Y, Y) - 1

            @pl.when(j >= 0)
            def _():
                ysend_c[k, j] = coupling_chunk(s).astype(BF16)
                y_copy(k, j, ysend_c, ybuf_c, ys_c, yr_c).start()

    loads[3].wait()
    coupling_part(layer)
    layer_wait(partner)
    coupling_part(partner)
    gbuf[me] = gpart[strip_of(me), :]

    def strip_wait(i):
        s = lax.rem(me + 1 + i, dp)
        send(gpart.at[strip_of(s)], gbuf.at[s], gs_send.at[i], gs_recv.at[s], dp=s).wait_recv()

    loop(dp - 1, strip_wait)
    summed = gbuf[0]
    for s in range(1, dp):
        summed = summed + gbuf[s]
    gfull[strip_of(me), :] = summed

    def full_copy(i):
        to = lax.rem(me + 1 + i, dp)
        return send(gfull.at[strip_of(me)], gfull.at[strip_of(me)], gg_send.at[i], gg_recv.at[me], dp=to)

    loop(dp - 1, lambda i: full_copy(i).start())

    def other_chip(i):
        b = same_core(i)
        layer_wait(b)
        layer_pass(i, lambda copy: copy.start())
        coupling_part(b)

    def other_chip_core(i):
        b = lax.rem(pair + 1 + i, pairs) * 2 + 1 - core
        layer_wait(b)
        coupling_part(b)

    loop(pairs - 1, other_chip)
    loop(pairs - 1, other_chip_core)

    def full_wait(i):
        s = lax.rem(me + 1 + i, dp)
        send(
            gfull.at[strip_of(s)], gfull.at[strip_of(s)], gg_send.at[i], gg_recv.at[s], dp=s
        ).wait_recv()

    loop(dp - 1, full_wait)
    aug[:, :rank] = gfull[...]
    aug[:, rank:] = (
        lax.broadcasted_iota(jnp.int32, (rank, rank), 0) == lax.broadcasted_iota(jnp.int32, (rank, rank), 1)
    ).astype(F32)

    panels = rank // PANEL

    def m_copy(k, i):
        return send(
            mall.at[layer, k], mall.at[layer, k], m_send.at[k, i], m_recv.at[layer, k],
            layer=lax.rem(layer + 1 + i, layers),
        )

    def rows_done(k, root, finished):
        factors = 1.0 / (root.astype(BF16).astype(F32) + damping) - 1.0 / damping
        mall[layer, k, 0] = finished.astype(BF16)
        mall[layer, k, 1] = (factors * finished).astype(BF16)
        loop(layers - 1, lambda i: m_copy(k, i).start())

    def factor_panels(first, last, found):
        return lax.fori_loop(first, last, lambda k, at: cholesky_step(k, at, aug, roots, rows_done), found)

    found = panel_factor(aug[:PANEL, :PANEL], PANEL)
    found = factor_panels(0, (panels - Z + 2) // 2, found)
    total = scatter_z(coupling_chunk, ysend_c, ybuf_c, ys_c, yr_c, zsend_c, zbuf_c, zs_c, zr_c)
    found = factor_panels((panels - Z + 2) // 2, panels - Z + 1, found)
    total = scatter_sum(total, zsend_c, zbuf_c, zs_c, zr_c)
    cfull[me] = total.astype(BF16)
    gather_start(cfull, cg)
    for dist in range(1, Z):
        found = factor_panels(panels - Z + dist, panels - Z + dist + 1, found)
        gather_stage(cfull, cg, dist)

    inverse = aug[:, :rank]
    eigen = roots[...].astype(BF16)
    on_diagonal = lax.broadcasted_iota(jnp.int32, (rank, rank), 0) == lax.broadcasted_iota(
        jnp.int32, (rank, rank), 1
    )
    eigen_ref[...] = jnp.sum(jnp.where(on_diagonal, eigen.astype(F32), 0.0), axis=0, keepdims=True)
    fresh_ref[...] = dot_nt(applied_ref[...], inverse, precision=HIGHEST).astype(BF16)
    gather_rows(cfull, cg, lambda s: None)

    def m_wait(i):
        b = lax.rem(layer + 1 + i, layers)
        for k in range(panels):
            send(mall.at[b, k], mall.at[b, k], m_send.at[k, i], m_recv.at[b, k], layer=b).wait_recv()

    loop(layers - 1, m_wait)

    gather_done(qfull, ag)
    scatter_done(ysend_a, ybuf_a, ys_a, yr_a, zsend_a, zbuf_a, zs_a, zr_a)
    layer_own(lambda copy: copy.wait_send())
    loop(pairs - 1, lambda i: layer_pass(i, lambda copy: copy.wait_send()))
    loop(dp - 1, lambda i: strip_copy(i).wait_send())
    loop(dp - 1, lambda i: full_copy(i).wait_send())
    scatter_done(ysend_c, ybuf_c, ys_c, yr_c, zsend_c, zbuf_c, zs_c, zr_c)
    gather_done(cfull, cg)
    for k in range(panels):
        loop(layers - 1, lambda i: m_copy(k, i).wait_send())


def per_device(layers, dp, acts, factor_old, basis_old, grads):
    Z = 4 if dp % 4 == 0 else 1
    Y = dp // Z
    tokens, width = acts.shape[1:]
    rows, rank = basis_old.shape[1:]
    blocks, _, cols = grads.shape
    chunk = blocks * rank // dp
    V, DMA = pltpu.VMEM, pltpu.SemaphoreType.DMA
    Y1, Z1, L1 = max(Y - 1, 1), max(Z - 1, 1), max(layers - 1, 1)
    scratch = [
        V((tokens, width), BF16),
        V((rows, width), BF16),
        V((blocks, rows, cols), BF16),
        V((dp, rows, rank), BF16),
        V((tokens, rank), F32),
        V((rows, rank), F32),
        V((Z, Y1, rows, rank), BF16),
        V((Z, Y1, rows, rank), BF16),
        V((Z1, rows, rank), BF16),
        V((Z1, rows, rank), BF16),
        V((rank, rank), F32),
        V((dp, rank // dp, rank), F32),
        V((rank, rank), F32),
        V((rank, 2 * rank), F32),
        V((rank, 1), F32),
        V((blocks * rank, cols), F32),
        V((Z, Y1, chunk, cols), BF16),
        V((Z, Y1, chunk, cols), BF16),
        V((Z1, chunk, cols), BF16),
        V((Z1, chunk, cols), BF16),
        DMA((4,)),
        DMA((2,)), DMA((Y1,)), DMA((2, Z1)), DMA((2, Z1, Y1)), DMA((dp,)),
        DMA((Z, Y1)), DMA((Z, Y1)), DMA((Z1,)), DMA((Z1,)),
        DMA((L1,)), DMA((layers,)),
        DMA((dp,)), DMA((dp,)), DMA((dp,)), DMA((dp,)),
        DMA((Z, Y1)), DMA((Z, Y1)), DMA((Z1,)), DMA((Z1,)),
        DMA((2,)), DMA((Y1,)), DMA((2, Z1)), DMA((2, Z1, Y1)), DMA((dp,)),
        DMA((rank // PANEL, L1)), DMA((layers, rank // PANEL)),
    ]
    vmem = pl.BlockSpec(memory_space=pltpu.VMEM)
    mall, cfull, appall, applied, new_basis, eigen = pl.pallas_call(
        functools.partial(kernel, layers, Z, Y, tokens * dp),
        out_shape=(
            jax.ShapeDtypeStruct((blocks, rank // PANEL, 2, PANEL, rank), BF16),
            jax.ShapeDtypeStruct((dp, chunk, cols), BF16),
            jax.ShapeDtypeStruct((blocks, rows, rank), BF16),
            jax.ShapeDtypeStruct((rows, rank), F32),
            jax.ShapeDtypeStruct((rows, rank), BF16),
            jax.ShapeDtypeStruct((1, rank), F32),
        ),
        in_specs=[pl.BlockSpec(memory_space=pltpu.HBM)] * 4,
        out_specs=(vmem,) * 6,
        scratch_shapes=scratch,
        compiler_params=pltpu.CompilerParams(
            collective_id=0, has_side_effects=True, vmem_limit_bytes=50 * 1024 * 1024
        ),
    )(acts, factor_old, basis_old, grads)
    per = rank // chunk
    by_block = lambda b: (b, 0, 0)
    whole = lambda b: (0, 0)
    conditioned, fresh, applied_rows, eigen = pl.pallas_call(
        functools.partial(finish_kernel, scale=math.sqrt(width)),
        grid=(blocks,),
        out_shape=(
            jax.ShapeDtypeStruct((blocks, rows, cols), BF16),
            jax.ShapeDtypeStruct((rows, rank), BF16),
            jax.ShapeDtypeStruct((rows, rank), F32),
            jax.ShapeDtypeStruct((1, rank), BF16),
        ),
        in_specs=[
            pl.BlockSpec((1, rank // PANEL, 2, PANEL, rank), lambda b: (b, 0, 0, 0, 0)),
            pl.BlockSpec((per, chunk, cols), by_block),
            pl.BlockSpec((1, rows, rank), by_block),
            pl.BlockSpec((1, rows, cols), by_block),
            pl.BlockSpec((rows, rank), whole),
            pl.BlockSpec((rows, rank), whole),
            pl.BlockSpec((1, rank), whole),
        ],
        out_specs=(
            pl.BlockSpec((1, rows, cols), by_block),
            pl.BlockSpec((rows, rank), whole),
            pl.BlockSpec((rows, rank), whole),
            pl.BlockSpec((1, rank), whole),
        ),
        compiler_params=pltpu.CompilerParams(vmem_limit_bytes=12 * 1024 * 1024),
    )(mall, cfull, appall, grads, applied, new_basis, eigen)
    return fresh[None], eigen, conditioned, applied_rows[None]


def solution(mesh):
    in_specs = (
        P("layer", "dp", None),
        P("layer", "dp", None),
        P("layer", "dp", None),
        P(None, "dp", "layer"),
    )
    out_specs = (
        P("layer", "dp", None),
        P("layer", None),
        P(None, "dp", "layer"),
        P("layer", "dp", None),
    )
    body = functools.partial(per_device, mesh.shape["layer"], mesh.shape["dp"])
    return jax.shard_map(body, mesh=mesh, in_specs=in_specs, out_specs=out_specs, check_vma=False)
```

time: 486 us -> 119 us (0.24)
  waiting for transfers between devices: 324 us -> 0 us
  Pallas kernels: 0 us -> 116 us
  other arithmetic: 71.1 us -> 0 us
  local copies, waits for them, and re-layouts: 43.1 us -> 2.31 us
  matrix products: 21.7 us -> 0 us
  between operations: 15.2 us -> 0.67 us
  starting transfers between devices: 9.25 us -> 0 us
    psum x2 -> x0, waiting for transfers between devices: 164 us -> none  [the longest x1 98.7 us: per_device(): coupling = lax.psum(coupling_local, 'dp')]
    pallas_call x0 -> x2, Pallas kernels: none -> 116 us  [the longest x1 112 us: per_device(): pl.pallas_call(functools.partial(kernel, layers, Z, Y, tokens * dp), out_...]
    reduce_scatter x1 -> x0, waiting for transfers between devices: 82.2 us -> none  [per_device(): lax.psum_scatter(lax.dot_general(token_rows, projected, (((0,), (0,)), ((...]
    all_gather x1 -> x0, waiting for transfers between devices: 54.2 us -> none  [per_device(): old_basis = lax.all_gather(basis_old, 'dp', axis=1, tiled=True)[0]]
    another operation x10 -> x0, other arithmetic: 53.8 us -> none  [the longest x6 34.1 us: per_device(): lower = jnp.linalg.cholesky(gram_total)]
    all_to_all x2 -> x0, waiting for transfers between devices: 23.5 us -> none  [the longest x1 23.5 us: per_device(): lax.all_to_all(result.astype(jnp.bfloat16)[None], 'layer', split_axis=2,...]
    dot_general x5 -> x0, matrix products: 19.8 us -> none  [the longest x1 5.95 us: per_device(): lax.dot_general(token_rows, projected, (((0,), (0,)), ((), ())), preferre...]
    unnamed x9 -> x6, local copies, waits for them, and re-layouts: 21 us -> 2.31 us
  transfers between devices with their start and end apart: 6 -> 0, of which waited for: 5 -> 0; matrix products, arithmetic and copies ran while one was open for 3% -> 0% of each run, Pallas kernels for 0% -> 0%
where the time goes in v1:
time: 119 us
  Pallas kernels  116 us (97%)
  local copies, waits for them, and re-layouts  2.31 us (2%)
    pallas_call x1, Pallas kernels, per_device(): pl.pallas_call(functools.partial(kernel, layers, Z, Y, tokens * dp), out_...  112 us
    pallas_call x1, Pallas kernels, per_device(): pl.pallas_call(functools.partial(finish_kernel, scale=math.sqrt(width)),...  3.99 us

profile of v1, /device:TPU:0, one launch (start us, length us, event | category | flops | bytes accessed | tf_op | source)
XLA Modules:
  0.0 118.6 jit_solution(15847687014649000287)
XLA Ops:
  0.6 0.0 copy-start
  0.6 0.0 copy-start.2
  0.7 1.1 copy-done.2
  1.7 111.7 %shard_map.75 = (bf16[4,8,2,32,256]{4,3,2,1,0:T(8,128)(2,1)S(1)}, bf16[8,128,512]{2,1,0:T(8,128)(2,1)S(1)}, bf16[4,512,256]{2,1,0:T(8,128)(2,1)}, f32[512,256]{1...) custom-call(bf16[1,256,4096]{2,1,0:T(8,128)(2,1)} %acts_hbm.1, bf16[1,512,4096]{2,1,0:T(8,128)(2,1)} %factor_hbm.1, ...), custom_call_target="tpu_custom_call" | custom-call | tf_op jit(solution)/shard_map/pallas_call | solution.py:557
  113.4 0.0 copy-done
  113.4 0.0 copy-start.1
  113.4 1.2 %copy-done.1 = bf16[4,512,256]{2,1,0:T(8,128)(2,1)S(1)} copy-done((bf16[4,512,256]{2,1,0:T(8,128)(2,1)S(1)}, bf16[4,512,256]{2,1,0:T(8,128)(2,1)}, u32[]{:S(2)}) %copy-start.1) | copy-done | bytes 1048600
  114.7 4.0 %shard_map.76 = (bf16[4,512,512]{2,1,0:T(8,128)(2,1)}, bf16[512,256]{1,0:T(8,128)(2,1)}, f32[512,256]{1,0:T(8,128)}, bf16[1,256]{1,0:T(2,128)(2,1)}) custom-call(bf16[4,8,2,32,256]{4,3,2,1,0:T(8,128)(2,1)S(1)} %get-tuple-element.14.mall, bf16[8,128,512]{2,1,0:T(8,128)(2,1)S(1)} %get-tuple-element.15.cfull, bf16[4,512,256]{2,1,0:T(8,128)(2,1)S(1)} %copy-done.1, ...), custom_call_target="tpu_custom_call" | custom-call | tf_op jit(solution)/shard_map/pallas_call | solution.py:577
Async XLA Ops:
  0.6 112.8 %copy-start = (bf16[4,512,512]{2,1,0:T(8,128)(2,1)S(1)}, bf16[4,512,512]{2,1,0:T(8,128)(2,1)}, u32[]{:S(2)}) copy-start(bf16[4,512,512]{2,1,0:T(8,128)(2,1)} %grads.1) | copy-start | bytes 6291460
  0.6 1.1 copy-start.2
  113.4 1.2 %copy-start.1 = (bf16[4,512,256]{2,1,0:T(8,128)(2,1)S(1)}, bf16[4,512,256]{2,1,0:T(8,128)(2,1)}, u32[]{:S(2)}) copy-start(bf16[4,512,256]{2,1,0:T(8,128)(2,1)} %get-tuple-element.16.appall) | copy-start | bytes 3145732

commit v2 on v1

--- a/solution.py
+++ b/solution.py
@@ -446,6 +446,8 @@
     loop(pairs - 1, other_chip)
     loop(pairs - 1, other_chip_core)
 
+    total = scatter_z(coupling_chunk, ysend_c, ybuf_c, ys_c, yr_c, zsend_c, zbuf_c, zs_c, zr_c)
+
     def full_wait(i):
         s = lax.rem(me + 1 + i, dp)
         send(
@@ -476,15 +478,14 @@
         return lax.fori_loop(first, last, lambda k, at: cholesky_step(k, at, aug, roots, rows_done), found)
 
     found = panel_factor(aug[:PANEL, :PANEL], PANEL)
-    found = factor_panels(0, (panels - Z + 2) // 2, found)
-    total = scatter_z(coupling_chunk, ysend_c, ybuf_c, ys_c, yr_c, zsend_c, zbuf_c, zs_c, zr_c)
-    found = factor_panels((panels - Z + 2) // 2, panels - Z + 1, found)
+    found = factor_panels(0, 1, found)
     total = scatter_sum(total, zsend_c, zbuf_c, zs_c, zr_c)
     cfull[me] = total.astype(BF16)
     gather_start(cfull, cg)
     for dist in range(1, Z):
-        found = factor_panels(panels - Z + dist, panels - Z + dist + 1, found)
+        found = factor_panels(dist, dist + 1, found)
         gather_stage(cfull, cg, dist)
+    found = factor_panels(Z, panels, found)
 
     inverse = aug[:, :rank]
     eigen = roots[...].astype(BF16)
@@ -568,7 +569,7 @@
         out_specs=(vmem,) * 6,
         scratch_shapes=scratch,
         compiler_params=pltpu.CompilerParams(
-            collective_id=0, has_side_effects=True, vmem_limit_bytes=50 * 1024 * 1024
+            collective_id=0, has_side_effects=True, vmem_limit_bytes=48 * 1024 * 1024
         ),
     )(acts, factor_old, basis_old, grads)
     per = rank // chunk

time: 119 us -> 119 us (level)
  local copies, waits for them, and re-layouts: 2.31 us -> 1.1 us
    pallas_call x1, Pallas kernels: 112 us -> 113 us  [per_device(): pl.pallas_call(functools.partial(kernel, layers, Z, Y, tokens * dp), out_...]
    unnamed x6 -> x4, local copies, waits for them, and re-layouts: 2.31 us -> 1.1 us
where the time goes in v2:
time: 119 us
  Pallas kernels  117 us (98%)
    pallas_call x1, Pallas kernels, per_device(): pl.pallas_call(functools.partial(kernel, layers, Z, Y, tokens * dp), out_...  113 us
    pallas_call x1, Pallas kernels, per_device(): pl.pallas_call(functools.partial(finish_kernel, scale=math.sqrt(width)),...  4.02 us

profile of v2, /device:TPU:0, one launch (start us, length us, event | category | flops | bytes accessed | tf_op | source)
XLA Modules:
  0.0 118.9 jit_solution(16771851130555738588)
XLA Ops:
  0.6 0.0 copy-start
  0.6 0.0 copy-start.1
  0.7 1.1 copy-done.1
  1.7 113.1 %shard_map.75 = (bf16[4,8,2,32,256]{4,3,2,1,0:T(8,128)(2,1)S(1)}, bf16[8,128,512]{2,1,0:T(8,128)(2,1)S(1)}, bf16[4,512,256]{2,1,0:T(8,128)(2,1)S(1)}, f32[512,25...) custom-call(bf16[1,256,4096]{2,1,0:T(8,128)(2,1)} %acts_hbm.1, bf16[1,512,4096]{2,1,0:T(8,128)(2,1)} %factor_hbm.1, ...), custom_call_target="tpu_custom_call" | custom-call | tf_op jit(solution)/shard_map/pallas_call | solution.py:558
  114.9 0.0 copy-done
  114.9 4.0 %shard_map.76 = (bf16[4,512,512]{2,1,0:T(8,128)(2,1)}, bf16[512,256]{1,0:T(8,128)(2,1)}, f32[512,256]{1,0:T(8,128)}, bf16[1,256]{1,0:T(2,128)(2,1)}) custom-call(bf16[4,8,2,32,256]{4,3,2,1,0:T(8,128)(2,1)S(1)} %get-tuple-element.14.mall, bf16[8,128,512]{2,1,0:T(8,128)(2,1)S(1)} %get-tuple-element.15.cfull, ...), custom_call_target="tpu_custom_call" | custom-call | tf_op jit(solution)/shard_map/pallas_call | solution.py:578
Async XLA Ops:
  0.6 114.3 %copy-start = (bf16[4,512,512]{2,1,0:T(8,128)(2,1)S(1)}, bf16[4,512,512]{2,1,0:T(8,128)(2,1)}, u32[]{:S(2)}) copy-start(bf16[4,512,512]{2,1,0:T(8,128)(2,1)} %grads.1) | copy-start | bytes 6291460
  0.6 1.1 copy-start.1
